TPU v7x, 32 devices: a whole 2x2x4 slice. The times are simulated.
32 devices in a mesh: seq: 16 (over z, y, core), tab: 2 (over x).
Axes of the slice: x: 2, y: 2, z: 4, core: 2. Of those that a mesh axis runs over, the one named last changes fastest.
Arguments:
- cotangent: bfloat16 [16384, 2560], P('seq', 'tab'), may hold values from -6 to 6
- saved_value: bfloat16 [16384, 2560], P('seq', 'tab'), may hold values from -6 to 6
- gate_scale: float32 [16384], P('seq'), may hold values from 0.2 to 1
- conv_weight: float32 [4, 2560], P(None, 'tab'), may hold values from -3 to 3
- value_weight: bfloat16 [1280, 2560], P(None, 'tab'), may hold values from -0.25 to 0.25
- owner_ids: int32 [8, 16384, 1], P('tab', 'seq'), may hold values from 0 to 15; in each aligned block of 1024 rows (0 to 1023, 1024 to 2047, ..., all dimensions but the last counted through in order) at most 256 rows name the same one
- local_row: int32 [8, 16384], P('tab', 'seq'), may hold values from 0 to 511
- row_table: float32 [8, 8192, 160], P('tab', 'seq'), may hold values from -6 to 6
- moment_one: float32 [8, 8192, 160], P('tab', 'seq'), may hold values from -6 to 6
- moment_two: float32 [8, 8192, 160], P('tab', 'seq'), may hold values from 0.5 to 4
Outputs:
- new_table: float32 [8, 8192, 160], P('tab', 'seq')
- new_first: float32 [8, 8192, 160], P('tab', 'seq')
- new_second: float32 [8, 8192, 160], P('tab', 'seq')
Inputs may be any that keep to these rules, and one draw needn't show every extreme that they name: `owner_ids`: within each aligned block of 1024 tokens of one head (one device's tokens), no owner is named by more than 256 tokens; in some blocks one owner is named by exactly 256.
All inputs are finite; a program needn't handle non-finite values.
Results may differ from a plain program's by a relative error of at most 0.0029.
Values may be sent and summed in bfloat16 or wider, within the bound.
A program may use at most 128 MiB of HBM per device.

v0:
```python
import jax
import jax.numpy as jnp
from jax import lax
from jax.sharding import PartitionSpec as P

beta_one = 0.9
beta_two = 0.95
learn_rate = 0.01
adam_steps = 10.0
epsilon = 1e-08


def from_behind(block, axis, distance):
    devices = range(lax.axis_size(axis))
    route = [(i - distance, i) for i in devices if i - distance in devices]
    return lax.ppermute(block, axis, route)


def causal_mix(context, conv_weight, length):
    mix_total = jnp.zeros((length, context.shape[1]), jnp.float32)
    for tap_index in range(4):
        row_start = 9 - 3 * tap_index
        mix_total = (
            mix_total + conv_weight[tap_index][None, :] * context[row_start : row_start + length]
        )
    return mix_total


def conv_adjoint(upstream, mixed_conv):
    squashed = jax.nn.sigmoid(mixed_conv)
    return upstream * squashed * (1.0 + mixed_conv * (1.0 - squashed))


def shards(
    cotangent,
    saved_value,
    gate_scale,
    conv_weight,
    value_weight,
    owner_ids,
    local_row,
    row_table,
    moment_one,
    moment_two,
):
    length = cotangent.shape[0]
    head_local = row_table.shape[0]
    table_rows = row_table.shape[1]
    head_dim = row_table.shape[2]
    own_width = head_local * head_dim
    peer_count = lax.axis_size("seq")
    count_cap = 4 * length // peer_count
    upstream = cotangent.astype(jnp.float32)
    value_rows = saved_value.astype(jnp.float32)
    prior_rows = from_behind(saved_value[length - 9 :], "seq", 1)
    context = jnp.concatenate([prior_rows.astype(jnp.float32), value_rows], axis=0)
    conv_grad = conv_adjoint(upstream, causal_mix(context, conv_weight, length))
    following = from_behind(conv_grad[:9], "seq", -1)
    extended = jnp.concatenate([conv_grad, following], axis=0)
    value_grad = upstream
    for tap_index in range(4):
        row_start = 3 * tap_index
        value_grad = (
            value_grad + conv_weight[tap_index][None, :] * extended[row_start : row_start + length]
        )
    scaled = (gate_scale[:, None] * value_grad).astype(jnp.bfloat16)
    full_term = lax.dot_general(
        value_weight, scaled, (((1,), (1,)), ((), ())), preferred_element_type=jnp.float32
    )
    summed = lax.psum(full_term, "tab")
    memory_grad = lax.dynamic_slice_in_dim(summed, lax.axis_index("tab") * own_width, own_width, 0)
    heads_grad = jnp.swapaxes(memory_grad.reshape(head_local, head_dim, length), 1, 2)
    owners = owner_ids[:, :, 0]
    position = jnp.arange(length, dtype=jnp.int32)
    earlier = position[None, :] < position[:, None]
    same_owner = owners[:, :, None] == owners[:, None, :]
    slot_rank = jnp.sum((same_owner & earlier[None]).astype(jnp.int32), axis=2)
    slot_index = owners * count_cap + slot_rank
    head_ids = jnp.broadcast_to(jnp.arange(head_local, dtype=jnp.int32)[:, None], slot_index.shape)
    send_grad = (
        jnp.zeros((head_local, peer_count * count_cap, head_dim), jnp.float32)
        .at[head_ids, slot_index]
        .set(heads_grad)
    )
    send_rows = (
        jnp.zeros((head_local, peer_count * count_cap), jnp.int32)
        .at[head_ids, slot_index]
        .set(local_row + 1)
    )
    send_grad = send_grad.reshape(head_local, peer_count, count_cap, head_dim)
    send_rows = send_rows.reshape(head_local, peer_count, count_cap)
    grads_in = lax.all_to_all(send_grad, "seq", split_axis=1, concat_axis=1, tiled=True)
    rows_in = lax.all_to_all(send_rows, "seq", split_axis=1, concat_axis=1, tiled=True)
    item_count = grads_in.shape[0]
    flat_rows = rows_in.reshape(item_count, -1) - 1
    flat_grads = grads_in.reshape(item_count, -1, head_dim)
    item_ids = jnp.broadcast_to(jnp.arange(item_count, dtype=jnp.int32)[:, None], flat_rows.shape)
    target = jnp.where(flat_rows < 0, table_rows, flat_rows)
    summed_rows = (
        jnp.zeros((item_count, table_rows, head_dim), jnp.float32)
        .at[item_ids, target]
        .add(flat_grads, mode="drop")
    )
    row_hits = (
        jnp.zeros((item_count, table_rows), jnp.int32).at[item_ids, target].add(1, mode="drop")
    )
    row_grad, row_hits = (summed_rows, row_hits)
    touched = (row_hits > 0)[:, :, None]
    first_next = beta_one * moment_one + (1.0 - beta_one) * row_grad
    second_next = beta_two * moment_two + (1.0 - beta_two) * row_grad * row_grad
    update = (
        first_next
        / (1.0 - beta_one**adam_steps)
        / (jnp.sqrt(second_next / (1.0 - beta_two**adam_steps)) + epsilon)
    )
    table_next = row_table - learn_rate * update
    return (
        jnp.where(touched, table_next, row_table),
        jnp.where(touched, first_next, moment_one),
        jnp.where(touched, second_next, moment_two),
    )


def solution(mesh):
    in_specs = (
        P("seq", "tab"),
        P("seq", "tab"),
        P("seq"),
        P(None, "tab"),
        P(None, "tab"),
        P("tab", "seq", None),
        P("tab", "seq"),
        P("tab", "seq", None),
        P("tab", "seq", None),
        P("tab", "seq", None),
    )
    out_specs = (P("tab", "seq", None), P("tab", "seq", None), P("tab", "seq", None))
    return jax.shard_map(shards, mesh=mesh, in_specs=in_specs, out_specs=out_specs, check_vma=False)
```

profile of v0, /device:TPU:9, one launch (start us, length us, event | category | flops | bytes accessed | tf_op | source)
XLA Modules:
  0.0 578.8 jit_solution(26141334458061464)
XLA Ops:
  7.2 0.0 copy-start
  7.2 0.0 all-reduce.2.cloned.1.call-start
  7.2 0.0 copy-start.3
  7.2 1.0 slice.42
  8.2 3.8 collective-permute-start
  12.0 0.9 slice_reduce_fusion.3
  13.0 2.1 convert_element_type.17
  15.1 0.0 collective-permute-done
  15.1 0.0 copy-done.3
  15.1 0.0 copy-start.10
  15.2 4.2 fusion.2
  19.4 0.0 copy-start.2
  19.4 2.3 copy-done.2
  21.7 2.0 collective-permute-start.1
  23.7 3.8 collective-permute-done.1
  27.5 0.0 copy-done
  27.5 0.0 copy-done.10
  27.5 17.3 %convolution_bitcast_fusion = f32[1280,1024]{0,1:T(8,128)} fusion(bf16[1280,1280]{1,0:T(8,128)(2,1)S(1)} %copy-done, bf16[1024,1280]{1,0:T(8,128)(2,1)} %param.10, f32[9,1280]{1,0:T(8,128)S(1)} %collective-permute-done.1, f32[1024,1280]{1,0:T(8,128)} %copy-done.2, f32[1280]{0:T(1024)S(1)} %get-tuple-element.20, f32[1280]{0:T(1024)S(1)} %get-tuple-element.21, ...), kind=kOutput, calls=%fused_computation.34 | convolution fusion | flops 3373793280 | bytes 16454656 | tf_op jit(solution)/shard_map/dot_general | solution.py:67
  44.7 0.0 copy-start.4
  44.7 0.0 copy-start.8
  44.7 0.0 copy-start.9
  44.7 0.0 copy-start.5
  44.8 0.0 all-reduce.2.cloned.1.call-update
  44.8 0.7 copy-done.4
  45.5 0.3 iota_compare_fusion
  45.8 3.6 convert_reduce_fusion
  49.4 0.0 copy-done.8
  49.4 0.1 multiply_reduce_fusion.1
  49.5 0.0 copy-done.9
  49.5 0.1 and_reduce_fusion.1
  49.6 0.0 copy-done.5
  49.7 15.6 %scatter_custom_fusion = s32[16384]{0:T(1024)S(1)} fusion(s32[4096]{0:T(1024)S(1)} %get-tuple-element.26, s32[4096]{0:T(1024)S(1)} %get-tuple-element.25, s32[]{:T(128)} %constant.19.clone.1), kind=kCustom, calls=%fused_computation.53 | custom fusion | bytes 65540
  65.2 0.7 copy.69
  65.9 5.9 %all-to-all-start = ((s32[4,16,256]{2,0,1:T(4,128)}), s32[4,16,256]{2,0,1:T(4,128)S(1)}, u32[]{:S(2)}, u32[]{:S(2)}) async-start(s32[4,16,256]{2,0,1:T(4,128)} %copy.69), calls=%async_computation | async-start | bytes 131072 | tf_op jit(solution)/shard_map/all_to_all | solution.py:93
  71.9 104.1 %all-reduce.2.cloned.1.call-done = f32[1280,1024]{0,1:T(8,128)} async-done(((f32[1280,1024]{0,1:T(8,128)}), f32[1280,1024]{0,1:T(8,128)}) %all-reduce.2.cloned.1.call-update) | async-done | bytes 5242896 | tf_op jit(solution)/shard_map/psum | solution.py:70
  176.0 1.9 constant_dynamic-slice_fusion
  177.9 2.1 copy.71
  180.0 4.7 copy.86
  184.7 24.6 %scatter_custom_fusion.2 = f32[16384,160]{1,0:T(8,128)} fusion(s32[4096]{0:T(1024)S(1)} %get-tuple-element.26, f32[4096,160]{1,0:T(8,128)} %bitcast.33, f32[]{:T(128)} %constant.26.clone.1), kind=kCustom, calls=%fused_computation.5 | custom fusion | bytes 10486272
  209.3 15.4 %copy.74 = f32[4,16,256,160]{2,3,0,1:T(8,128)} copy(f32[4,16,256,160]{3,2,1,0:T(8,128)} %bitcast.29) | data formatting | bytes 20971520 | tf_op jit(solution)/shard_map/reshape | solution.py:90
  224.7 0.0 copy-start.7
  224.7 0.0 copy-start.6
  224.7 0.0 all-to-all-done
  224.8 6.5 %all-to-all-start.1 = ((f32[4,16,256,160]{2,3,0,1:T(8,128)}), f32[4,16,256,160]{2,3,0,1:T(8,128)}, u32[]{:S(2)}, u32[]{:S(2)}) async-start(f32[4,16,256,160]{2,3,0,1:T(8,128)} %copy.74), calls=%async_computation.1 | async-start | bytes 20971520 | tf_op jit(solution)/shard_map/all_to_all | solution.py:92
  231.3 0.0 copy-done.7
  231.4 0.1 multiply_reduce_fusion
  231.5 0.0 copy-done.6
  231.5 0.1 and_reduce_fusion
  231.7 87.3 %scatter_custom_fusion.1 = s32[2048]{0:T(1024)S(1)} fusion(s32[16384]{0:T(1024)S(1)} %bitcast.36, s32[16384]{0:T(1024)S(1)} %broadcast.161, s32[]{:T(128)} %constant.19.clone.1), kind=kCustom, calls=%fused_computation.69 | custom fusion | flops 16384 | bytes 8196
  319.0 137.4 %all-to-all-done.1 = f32[4,16,256,160]{2,3,0,1:T(8,128)} async-done(((f32[4,16,256,160]{2,3,0,1:T(8,128)}), f32[4,16,256,160]{2,3,0,1:T(8,128)}, u32[]{:S(2)}, u32[]{:S(2)}) %all-to-all-start.1) | async-done | bytes 10485792 | tf_op jit(solution)/shard_map/all_to_all | solution.py:92
  456.4 14.4 %copy.87 = f32[4,16,256,160]{3,2,1,0:T(8,128)} copy(f32[4,16,256,160]{2,3,0,1:T(8,128)} %all-to-all-done.1) | data formatting | bytes 20971520 | tf_op jit(solution)/shard_map/reshape | solution.py:96
  470.9 88.8 %scatter_custom_fusion.3 = f32[2048,160]{1,0:T(8,128)S(1)} fusion(s32[16384]{0:T(1024)S(1)} %bitcast.37, f32[16384,160]{1,0:T(8,128)} %bitcast.30, f32[]{:T(128)} %constant.26.clone.1), kind=kCustom, calls=%fused_computation.43 | custom fusion | flops 2621440 | bytes 1311232
  559.7 1.6 copy.88
  561.3 0.0 copy-start.1
  561.3 6.2 %copy_select_fusion = (f32[4,512,160]{1,0,2:T(4,128)S(1)}, f32[4,512,160]{1,0,2:T(4,128)S(1)}, f32[4,512,160]{1,0,2:T(4,128)S(1)}) fusion(f32[4,512,160]{1,2,0:T(8,128)} %param.19, f32[4,512,160]{1,0,2:T(4,128)} %copy.88, pred[4,512]{1,0:T(4,128)(4,1)S(1)} %reshape.109, f32[4,512,160]{1,2,0:T(8,128)} %param.18, f32[4,512,160]{1,2,0:T(8,128)} %param.17), kind=kLoop, calls=%fused_computation.41 | loop fusion | flops 5242880 | bytes 9177088 | tf_op jit(solution)/shard_map/jit(_where)/select_n | solution.py:120
  567.5 1.5 copy.83
  569.0 1.5 copy.84
  570.5 1.5 copy.85
  571.9 0.0 copy-done.1
  (17 shorter events, 0.2 us)
Async XLA Ops:
  7.2 20.3 %copy-start = (bf16[1280,1280]{1,0:T(8,128)(2,1)S(1)}, bf16[1280,1280]{1,0:T(8,128)(2,1)}, u32[]{:S(2)}) copy-start(bf16[1280,1280]{1,0:T(8,128)(2,1)} %param.14) | copy-start | bytes 9830404
  7.2 168.8 %all-reduce.2.cloned.1.call-start = ((), (), s32[]{:S(2)}) async-start(), calls=%async_computation.2 | async-start | bytes 10485760 | tf_op jit(solution)/shard_map/psum | solution.py:70
  7.2 7.9 %copy-start.3 = (bf16[1024,1280]{1,0:T(8,128)(2,1)S(1)}, bf16[1024,1280]{1,0:T(8,128)(2,1)}, u32[]{:S(2)}) copy-start(bf16[1024,1280]{1,0:T(8,128)(2,1)} %param.10) | copy-start | bytes 7864324
  8.2 6.9 %collective-permute-start = (bf16[9,1280]{1,0:T(8,128)(2,1)S(1)}, bf16[9,1280]{1,0:T(8,128)(2,1)S(1)}, u32[]{:S(2)}, u32[]{:S(2)}) collective-permute-start(bf16[9,1280]{1,0:T(8,128)(2,1)S(1)} %slice.42), channel_id=1, source_target_pairs={{0,2},{2,4},{4,6},{6,8},{8,10},{10,12},{12,14},{14,16},{16,18},{18... | collective-permute-start | bytes 69128 | tf_op jit(solution)/shard_map/ppermute | solution.py:16
  15.1 12.3 %copy-start.10 = (f32[1024]{0:T(1024)S(1)}, f32[1024]{0:T(1024)}, u32[]{:S(2)}) copy-start(f32[1024]{0:T(1024)} %param.12) | copy-start | bytes 12292
  19.4 2.3 copy-start.2
  21.7 5.7 collective-permute-start.1
  44.7 0.7 copy-start.4
  44.7 4.7 copy-start.8
  44.7 4.8 copy-start.9
  44.7 4.9 copy-start.5
  65.9 158.8 %all-to-all-start = ((s32[4,16,256]{2,0,1:T(4,128)}), s32[4,16,256]{2,0,1:T(4,128)S(1)}, u32[]{:S(2)}, u32[]{:S(2)}) async-start(s32[4,16,256]{2,0,1:T(4,128)} %copy.69), calls=%async_computation | async-start | bytes 131072 | tf_op jit(solution)/shard_map/all_to_all | solution.py:93
  224.7 6.6 %copy-start.7 = (s32[2]{0:T(128)S(1)}, s32[2]{0:T(128)}, u32[]{:S(2)}) copy-start(s32[2]{0:T(128)} %constant.58) | copy-start | bytes 28
  224.7 6.7 %copy-start.6 = (s32[2]{0:T(128)S(1)}, s32[2]{0:T(128)}, u32[]{:S(2)}) copy-start(s32[2]{0:T(128)} %constant.61) | copy-start | bytes 28
  224.8 231.7 %all-to-all-start.1 = ((f32[4,16,256,160]{2,3,0,1:T(8,128)}), f32[4,16,256,160]{2,3,0,1:T(8,128)}, u32[]{:S(2)}, u32[]{:S(2)}) async-start(f32[4,16,256,160]{2,3,0,1:T(8,128)} %copy.74), calls=%async_computation.1 | async-start | bytes 20971520 | tf_op jit(solution)/shard_map/all_to_all | solution.py:92
  561.3 10.6 %copy-start.1 = (bf16[1280,1280]{1,0:T(8,128)(2,1)S(1)}, bf16[1280,1280]{1,0:T(8,128)(2,1)}, u32[]{:S(2)}) copy-start(bf16[1280,1280]{1,0:T(8,128)(2,1)} %param.14) | copy-start | bytes 9830404
Sparse Core Ops, SparseCore 0:
  44.9 131.0 all-reduce.1
where the time goes:
time: 582 us; the launch traced here: 579 us
  waiting for transfers between devices  245 us (42%)
  other arithmetic  193 us (33%)
  local copies, waits for them, and re-layouts  90.4 us (16%)
  starting transfers between devices  18.3 us (3%)
  matrix products  17.3 us (3%)
  between operations  14.3 us (2%)
    unnamed x9, other arithmetic  177 us
    all_to_all x1, waiting for transfers between devices, shards(): lax.all_to_all(send_grad, 'seq', split_axis=1, concat_axis=1, tiled=True)  137 us
    psum x1, waiting for transfers between devices, shards(): summed = lax.psum(full_term, 'tab')  104 us
    unnamed x30, local copies, waits for them, and re-layouts  47.6 us
    dot_general x1, matrix products, shards(): lax.dot_general(value_weight, scaled, (((1,), (1,)), ((), ())), preferred...  17.3 us
    reshape x1, local copies, waits for them, and re-layouts, shards(): send_grad = send_grad.reshape(head_local, peer_count, count_cap, head_dim)  15.4 us
    reshape x1, local copies, waits for them, and re-layouts, shards(): flat_grads = grads_in.reshape(item_count, -1, head_dim)  14.4 us
  transfers between devices with their start and end apart: 5, of which 3 were waited for; matrix products, arithmetic and copies ran while one was open for 28% of the time, Pallas kernels for 0%

commit v1 on v0

v1 whole, which is shorter than its diff:
```python
import functools

import jax
import jax.numpy as jnp
from jax import lax
from jax.experimental import pallas as pl
from jax.experimental.pallas import tpu as pltpu
from jax.sharding import PartitionSpec as P

beta_one = 0.9
beta_two = 0.95
learn_rate = 0.01
adam_steps = 10.0
epsilon = 1e-08
HALO = 16
GROUP = 4
ROWS_TILE = 128
LANES = 128
CONTRACT_LAST = (((1,), (1,)), ((), ()))


def shifted(block, axis, distance):
    devices = range(lax.axis_size(axis))
    return lax.ppermute(block, axis, [(i, i + distance) for i in devices if i + distance in devices])


def flipped(block, axis, bit):
    return lax.ppermute(block, axis, [(i, i ^ bit) for i in range(lax.axis_size(axis))])


def project_kernel(
    heads, tabs, me_ref, cot_ref, sv_ref, prior_ref, next_cot_ref, next_sv_ref, gate_ref, taps_ref, w_ref, *rest
):
    own_refs, send_refs = rest[:heads], rest[heads : heads * tabs]
    cot_ext, sv_ext, scaled = rest[heads * tabs :]
    step = pl.program_id(0)
    length, width = cot_ref.shape
    f32 = jnp.float32
    sv_ext[:HALO] = prior_ref[...].astype(f32)
    sv_ext[HALO : HALO + length] = sv_ref[...].astype(f32)
    sv_ext[HALO + length :] = next_sv_ref[...].astype(f32)
    cot_ext[:length] = cot_ref[...].astype(f32)
    cot_ext[length:] = next_cot_ref[...].astype(f32)

    for lane in range(0, width, LANES):
        lanes = pl.ds(lane, LANES)
        taps = [taps_ref[k : k + 1, lanes] for k in range(4)]

        @pl.loop(0, length // ROWS_TILE)
        def _(tile):
            start = pl.multiple_of(tile * ROWS_TILE, ROWS_TILE)
            reach = ROWS_TILE + HALO
            context = sv_ext[pl.ds(start, reach + HALO), lanes]
            upstream = cot_ext[pl.ds(start, reach), lanes]
            mixed = taps[0] * context[HALO:]
            for k in range(1, 4):
                mixed = mixed + taps[k] * context[HALO - 3 * k : HALO - 3 * k + reach]
            squashed = 1.0 / (1.0 + jnp.exp(-mixed))
            grad = upstream * squashed * (1.0 + mixed * (1.0 - squashed))
            total = upstream[:ROWS_TILE]
            for k in range(4):
                total = total + taps[k] * grad[3 * k : 3 * k + ROWS_TILE]
            total = gate_ref[pl.ds(start, ROWS_TILE), :] * total
            column = pl.multiple_of(step * width + lane, LANES)
            scaled[pl.ds(start, ROWS_TILE), pl.ds(column, LANES)] = total.astype(jnp.bfloat16)

    @pl.when(step == pl.num_programs(0) - 1)
    def _():
        head_dim = own_refs[0].shape[0]
        for away in range(tabs):
            owner = lax.rem(me_ref[0] + away, tabs)
            for head in range(heads):
                first = pl.multiple_of((owner * heads + head) * head_dim, 32)
                part = lax.dot_general(
                    w_ref[pl.ds(first, head_dim), :], scaled[...], CONTRACT_LAST, preferred_element_type=f32
                )
                if away == 0:
                    own_refs[head][...] = part
                else:
                    send_refs[(away - 1) * heads + head][...] = part.astype(jnp.bfloat16)


def project(cotangent, saved_value, prior, next_cot, next_sv, gate, taps, weight, heads, tabs):
    length, features = cotangent.shape
    memory = weight.shape[0]
    head_dim = memory // (heads * tabs)
    width = next(w for w in (256, 128, features) if features % w == 0)
    own = [jax.ShapeDtypeStruct((head_dim, length), jnp.float32)] * heads
    send = [jax.ShapeDtypeStruct((head_dim, length), jnp.bfloat16)] * (heads * (tabs - 1))
    feature_block = lambda rows: pl.BlockSpec((rows, width), lambda i, me: (0, i))
    whole = lambda shape: pl.BlockSpec(shape, lambda i, me: (0, 0))
    outs = pl.pallas_call(
        functools.partial(project_kernel, heads, tabs),
        out_shape=own + send,
        grid_spec=pltpu.PrefetchScalarGridSpec(
            num_scalar_prefetch=1,
            grid=(features // width,),
            in_specs=[
                feature_block(length),
                feature_block(length),
                feature_block(HALO),
                feature_block(HALO),
                feature_block(HALO),
                whole((length, 1)),
                feature_block(4),
                whole(weight.shape),
            ],
            out_specs=[whole((head_dim, length))] * (heads * tabs),
            scratch_shapes=[
                pltpu.VMEM((length + HALO, width), jnp.float32),
                pltpu.VMEM((length + 2 * HALO, width), jnp.float32),
                pltpu.VMEM((length, features), jnp.bfloat16),
            ],
        ),
        compiler_params=pltpu.CompilerParams(vmem_limit_bytes=48 * 1024 * 1024),
        cost_estimate=pl.CostEstimate(
            flops=2 * length * features * memory, bytes_accessed=16 * 1024 * 1024, transcendentals=length * features
        ),
    )(lax.axis_index("tab")[None].astype(jnp.int32), cotangent, saved_value, prior, next_cot, next_sv, gate, taps, weight)
    return outs[:heads], [outs[heads * k : heads * (k + 1)] for k in range(1, tabs)]


def exchange_kernel(heads, tabs, planes, *refs):
    own_refs, send_refs = refs[:heads], refs[heads : heads * tabs]
    place_ref, sums_ref, hits_ref = refs[heads * tabs : heads * tabs + 3]
    (
        tab_in, mine, core_in, side_in, diag_in, table_out, table_in, count_out, count_in,
        tab_sems, core_sems, side_sems, diag_sems, table_sems, count_sems,
    ) = refs[heads * tabs + 3 :]
    head_dim, length = own_refs[0].shape
    rows = sums_ref.shape[2]
    seq, tab = lax.axis_index("seq"), lax.axis_index("tab")
    plane, column = seq // GROUP, seq % GROUP
    core = seq + 1 - 2 * (seq % 2)
    side = seq + 2 - 4 * ((seq // 2) % 2)
    tab_peer = lambda k: lax.rem(tab + k, tabs)
    plane_peer = lambda k: lax.rem(plane + k, planes) * GROUP + column

    count_out[...] = jnp.zeros_like(count_out)
    barrier = pltpu.get_barrier_semaphore()

    def greet(**place):
        pl.semaphore_signal(barrier, inc=1, device_id=place, device_id_type=pl.DeviceIdType.MESH)

    for k in range(1, tabs):
        greet(tab=tab_peer(k))
    greet(seq=core)
    greet(seq=side)
    for k in range(1, planes):
        greet(seq=plane_peer(k))
    pl.semaphore_wait(barrier, tabs + planes)

    def copy(source, target, sems, place):
        return pltpu.make_async_remote_copy(
            src_ref=source,
            dst_ref=target,
            send_sem=sems.at[0],
            recv_sem=sems.at[1],
            device_id=place,
            device_id_type=pl.DeviceIdType.MESH,
        )

    tab_copy = lambda k, h: copy(
        send_refs[(k - 1) * heads + h], tab_in.at[k - 1, h], tab_sems.at[k - 1, h], {"tab": tab_peer(k)}
    )
    core_copy = lambda h: copy(mine.at[h], core_in.at[h], core_sems.at[h], {"seq": core})
    side_copy = lambda h: copy(mine.at[h], side_in.at[h], side_sems.at[h], {"seq": side})
    diag_copy = lambda h: copy(side_in.at[h], diag_in.at[h], diag_sems.at[h], {"seq": core})
    table_copy = lambda k, h: copy(
        table_out.at[h, k - 1], table_in.at[h, k - 1], table_sems.at[h, k - 1], {"seq": plane_peer(k)}
    )
    count_copy = lambda k: copy(count_out.at[k], count_in.at[k - 1], count_sems.at[k - 1], {"seq": plane_peer(k)})

    for h in range(heads):
        for k in range(1, tabs):
            tab_copy(k, h).start()

    def combine(h):
        total = own_refs[h][...]
        for k in range(1, tabs):
            tab_copy(k, h).wait_recv()
            total = total + tab_in[k - 1, h].astype(jnp.float32)
        mine[h] = total.astype(jnp.bfloat16)
        side_copy(h).start()
        core_copy(h).start()

    def forward(h):
        side_copy(h).wait_recv()
        diag_copy(h).start()

    def add_up(h):
        core_copy(h).wait_recv()
        diag_copy(h).wait_recv()
        row = lax.broadcasted_iota(jnp.int32, (rows, length), 0)
        ones = jnp.ones((16, length), jnp.bfloat16)

        def sums_of(away):
            total = jnp.zeros((head_dim + 16, rows), jnp.float32)
            for source, held in enumerate((mine, core_in, side_in, diag_in)):
                place = place_ref[h * GROUP + source : h * GROUP + source + 1, :] - away * rows
                chosen = (place == row).astype(jnp.float32).astype(jnp.bfloat16)
                grads = jnp.concatenate([held[h], ones], axis=0)
                total = total + lax.dot_general(grads, chosen, CONTRACT_LAST, preferred_element_type=jnp.float32)
            return total

        @pl.loop(1, planes)
        def _(away):
            total = sums_of(away)
            table_out[h, away - 1] = total[:head_dim].astype(jnp.bfloat16)
            count_out[away, h : h + 1] = total[head_dim : head_dim + 1]
            table_copy(away, h).start()

        total = sums_of(0)
        sums_ref[h] = total[:head_dim]
        count_out[0, h : h + 1] = total[head_dim : head_dim + 1]

    combine(0)
    for h in range(heads):
        if h + 1 < heads:
            combine(h + 1)
        forward(h)
        add_up(h)

    for k in range(1, planes):
        count_copy(k).start()
    for h in range(heads):
        total = sums_ref[h]
        for k in range(1, planes):
            table_copy(k, h).wait_recv()
            total = total + table_in[h, k - 1].astype(jnp.float32)
        sums_ref[h] = total
    counts = count_out[0]
    for k in range(1, planes):
        count_copy(k).wait_recv()
        counts = counts + count_in[k - 1]
    hits_ref[...] = counts
    for h in range(heads):
        for k in range(1, tabs):
            tab_copy(k, h).wait_send()
        side_copy(h).wait_send()
        core_copy(h).wait_send()
        diag_copy(h).wait_send()
        for k in range(1, planes):
            table_copy(k, h).wait_send()
    for k in range(1, planes):
        count_copy(k).wait_send()


def exchange(own, send, places, rows, tabs, planes):
    heads = len(own)
    head_dim, length = own[0].shape
    vmem = pl.BlockSpec(memory_space=pltpu.VMEM)
    block = (head_dim, length)
    count_rows = -(-heads // 8) * 8
    pairs = lambda *shape: pltpu.SemaphoreType.DMA((*shape, 2))
    return pl.pallas_call(
        functools.partial(exchange_kernel, heads, tabs, planes),
        out_shape=[
            jax.ShapeDtypeStruct((heads, head_dim, rows), jnp.float32),
            jax.ShapeDtypeStruct((count_rows, rows), jnp.float32),
        ],
        in_specs=[vmem] * (heads * tabs + 1),
        out_specs=[vmem, vmem],
        scratch_shapes=[
            pltpu.VMEM((max(tabs - 1, 1), heads, *block), jnp.bfloat16),
            pltpu.VMEM((heads, *block), jnp.bfloat16),
            pltpu.VMEM((heads, *block), jnp.bfloat16),
            pltpu.VMEM((heads, *block), jnp.bfloat16),
            pltpu.VMEM((heads, *block), jnp.bfloat16),
            pltpu.VMEM((heads, planes - 1, head_dim, rows), jnp.bfloat16),
            pltpu.VMEM((heads, planes - 1, head_dim, rows), jnp.bfloat16),
            pltpu.VMEM((planes, count_rows, rows), jnp.float32),
            pltpu.VMEM((planes - 1, count_rows, rows), jnp.float32),
            pairs(max(tabs - 1, 1), heads),
            pairs(heads),
            pairs(heads),
            pairs(heads),
            pairs(heads, planes - 1),
            pairs(planes - 1),
        ],
        compiler_params=pltpu.CompilerParams(
            vmem_limit_bytes=52 * 1024 * 1024, collective_id=0, has_side_effects=True
        ),
        cost_estimate=pl.CostEstimate(
            flops=2 * planes * heads * GROUP * length * rows * 256, bytes_accessed=8 * 1024 * 1024, transcendentals=0
        ),
    )(*own, *send, places)


def shards(
    cotangent,
    saved_value,
    gate_scale,
    conv_weight,
    value_weight,
    owner_ids,
    local_row,
    row_table,
    moment_one,
    moment_two,
):
    length = cotangent.shape[0]
    heads, rows, head_dim = row_table.shape
    seqs, tabs = lax.axis_size("seq"), lax.axis_size("tab")
    planes = seqs // GROUP
    me = lax.axis_index("seq")
    plane, column = me // GROUP, me % GROUP

    prior = shifted(saved_value[length - HALO :], "seq", 1)
    next_rows = shifted(jnp.stack([cotangent[:HALO], saved_value[:HALO]]), "seq", -1)

    owners = owner_ids[:, :, 0]
    ids = owners * rows + local_row
    core_ids = flipped(ids, "seq", 1)
    side_ids = flipped(ids, "seq", 2)
    diag_ids = flipped(ids, "seq", 3)
    group_ids = jnp.stack([ids, core_ids, side_ids, diag_ids], axis=1)
    owner = group_ids // rows
    away = (owner // GROUP + planes - plane) % planes
    places = jnp.where(owner % GROUP == column, away * rows + group_ids % rows, -1)

    own, send = project(
        cotangent,
        saved_value,
        prior,
        next_rows[0],
        next_rows[1],
        gate_scale[:, None],
        conv_weight,
        value_weight,
        heads,
        tabs,
    )
    row_grad, hits = exchange(
        own, [part for parts in send for part in parts], places.reshape(heads * GROUP, length), rows, tabs, planes
    )
    touched = (hits[:heads] > 0)[:, None, :]
    turned = lambda array: jnp.swapaxes(array, 1, 2)
    table, first, second = turned(row_table), turned(moment_one), turned(moment_two)
    first_next = beta_one * first + (1.0 - beta_one) * row_grad
    second_next = beta_two * second + (1.0 - beta_two) * row_grad * row_grad
    update = (
        first_next
        / (1.0 - beta_one**adam_steps)
        / (jnp.sqrt(second_next / (1.0 - beta_two**adam_steps)) + epsilon)
    )
    table_next = table - learn_rate * update
    return (
        turned(jnp.where(touched, table_next, table)),
        turned(jnp.where(touched, first_next, first)),
        turned(jnp.where(touched, second_next, second)),
    )


def solution(mesh):
    in_specs = (
        P("seq", "tab"),
        P("seq", "tab"),
        P("seq"),
        P(None, "tab"),
        P(None, "tab"),
        P("tab", "seq", None),
        P("tab", "seq"),
        P("tab", "seq", None),
        P("tab", "seq", None),
        P("tab", "seq", None),
    )
    out_specs = (P("tab", "seq", None), P("tab", "seq", None), P("tab", "seq", None))
    return jax.shard_map(shards, mesh=mesh, in_specs=in_specs, out_specs=out_specs, check_vma=False)
```

time: 582 us -> 130 us (0.22)
  waiting for transfers between devices: 245 us -> 2.6 us
  other arithmetic: 193 us -> 5.5 us
  Pallas kernels: 0 us -> 105 us
  local copies, waits for them, and re-layouts: 90.4 us -> 5.92 us
  matrix products: 17.3 us -> 0 us
  between operations: 14.3 us -> 0.83 us
  starting transfers between devices: 18.3 us -> 7.53 us
    unnamed x9 -> x0, other arithmetic: 177 us -> none
    all_to_all x2 -> x0, waiting for transfers between devices: 137 us -> none  [the longest x1 137 us: shards(): lax.all_to_all(send_grad, 'seq', split_axis=1, concat_axis=1, tiled=True)]
    pallas_call x0 -> x2, Pallas kernels: none -> 105 us  [the longest x1 86.5 us: exchange(): pl.pallas_call(functools.partial(exchange_kernel, heads, tabs, planes), o...]
    psum x1 -> x0, waiting for transfers between devices: 104 us -> none  [shards(): summed = lax.psum(full_term, 'tab')]
    unnamed x30 -> x16, local copies, waits for them, and re-layouts: 47.6 us -> 3.35 us
    reshape x4 -> x0, local copies, waits for them, and re-layouts: 30.6 us -> none  [the longest x1 15.4 us: shards(): send_grad = send_grad.reshape(head_local, peer_count, count_cap, head_dim)]
    dot_general x1 -> x0, matrix products: 17.3 us -> none  [shards(): lax.dot_general(value_weight, scaled, (((1,), (1,)), ((), ())), preferred...]
    all_to_all x2 -> x0, starting transfers between devices: 12.5 us -> none  [the longest x1 6.53 us: shards(): lax.all_to_all(send_grad, 'seq', split_axis=1, concat_axis=1, tiled=True)]
  transfers between devices with their start and end apart: 5 -> 5, of which waited for: 3 -> 1; matrix products, arithmetic and copies ran while one was open for 28% -> 2% of each run, Pallas kernels for 0% -> 0%
where the time goes in v1:
time: 130 us; the launch traced here: 128 us
  Pallas kernels  105 us (81%)
  starting transfers between devices  7.53 us (6%)
  local copies, waits for them, and re-layouts  5.92 us (5%)
  other arithmetic  5.5 us (4%)
  waiting for transfers between devices  2.6 us (2%)
    pallas_call x1, Pallas kernels, exchange(): pl.pallas_call(functools.partial(exchange_kernel, heads, tabs, planes), o...  86.5 us
    pallas_call x1, Pallas kernels, project(): pl.pallas_call(functools.partial(project_kernel, heads, tabs), out_shape=...  18.8 us
    ppermute x2, starting transfers between devices, shifted(): lax.ppermute(block, axis, [(i, i + distance) for i in devices if i + dist...  5.2 us
    transpose x1, other arithmetic, shards(): turned = lambda array: jnp.swapaxes(array, 1, 2)  4.57 us
    unnamed x16, local copies, waits for them, and re-layouts  3.35 us
  transfers between devices with their start and end apart: 5, of which 1 were waited for; matrix products, arithmetic and copies ran while one was open for 2% of the time, Pallas kernels for 0%

profile of v1, /device:TPU:9, one launch (start us, length us, event | category | flops | bytes accessed | tf_op | source)
XLA Modules:
  0.0 127.7 jit_solution(13292289272858458416)
XLA Ops:
  0.6 0.0 copy-start
  0.6 0.7 bitcast_add_fusion
  1.4 1.9 %collective-permute-start.4 = (s32[4,1024]{1,0:T(4,128)S(1)}, s32[4,1024]{1,0:T(4,128)S(1)}, u32[]{:S(2)}, u32[]{:S(2)}) collective-permute-start(s32[4,1024]{1,0:T(4,128)S(1)} %bitcast_add_fusion), channel_id=1, source_target_pairs={{0,6},{2,4},{4,2},{6,0},{8,14},{10,12},{12,10},{14,8},{16,22},{18,... | collective-permute-start | bytes 49160 | tf_op jit(solution)/shard_map/ppermute | solution.py:28
  3.2 0.2 collective-permute-start.3
  3.5 0.2 collective-permute-start.2
  3.7 0.8 slice_bitcast_fusion.2
  4.5 3.3 %collective-permute-start = (bf16[16,1280]{1,0:T(8,128)(2,1)S(1)}, bf16[16,1280]{1,0:T(8,128)(2,1)S(1)}, u32[]{:S(2)}, u32[]{:S(2)}) collective-permute-start(bf16[16,1280]{1,0:T(8,128)(2,1)S(1)} %get-tuple-element.27), channel_id=1, source_target_pairs={{0,2},{2,4},{4,6},{6,8},{8,10},{10,12},{12,14},{14,16},{16,18},{18... | collective-permute-start | bytes 122888 | tf_op jit(solution)/shard_map/ppermute | solution.py:24
  7.8 0.8 slice_bitcast_fusion.3
  8.6 1.9 %collective-permute-start.1 = (bf16[2,16,1280]{2,1,0:T(8,128)(2,1)S(1)}, bf16[2,16,1280]{2,1,0:T(8,128)(2,1)S(1)}, u32[]{:S(2)}, u32[]{:S(2)}) collective-permute-start(bf16[2,16,1280]{2,1,0:T(8,128)(2,1)S(1)} %pad_maximum_fusion), channel_id=1, source_target_pairs={{2,0},{4,2},{6,4},{8,6},{10,8},{12,10},{14,12},{16,14},{18,16},{20... | collective-permute-start | bytes 245768 | tf_op jit(solution)/shard_map/ppermute | solution.py:24
  10.6 0.9 copy.15.gate_ref
  11.5 0.0 collective-permute-done.4
  11.5 0.0 collective-permute-done.3
  11.5 0.0 collective-permute-done.2
  11.6 0.2 fusion.11.refs_8_
  11.8 2.6 %collective-permute-done.1 = bf16[2,16,1280]{2,1,0:T(8,128)(2,1)S(1)} collective-permute-done((bf16[2,16,1280]{2,1,0:T(8,128)(2,1)S(1)}, bf16[2,16,1280]{2,1,0:T(8,128)(2,1)S(1)}, u32[]{:S(2)}, u32[]{:S(2)}) %collective-permute-start.1) | collective-permute-done | bytes 81952 | tf_op jit(solution)/shard_map/ppermute | solution.py:24
  14.4 0.0 collective-permute-done.prior_ref
  14.4 0.0 copy-done
  14.4 18.8 %shard_map.121 = (f32[160,1024]{1,0:T(8,128)S(1)}, f32[160,1024]{1,0:T(8,128)S(1)}, f32[160,1024]{1,0:T(8,128)S(1)}, f32[160,1024]{1,0:T(8,128)S(1)}, bf16[160,1...) custom-call(s32[1]{0:T(128)} %bitcast.me_ref, ...), custom_call_target="tpu_custom_call" | custom-call | flops 3355443200 | bytes 16777216 | tf_op jit(solution)/shard_map/pallas_call | solution.py:92
  33.2 0.0 copy-start.1
  33.2 0.8 copy-done.1
  34.1 0.0 copy-start.2
  34.1 0.8 copy-done.2
  34.9 0.0 copy-start.3
  34.9 0.8 copy-done.3
  35.7 0.0 copy-start.4
  35.7 0.8 copy-done.4
  36.6 0.0 copy-start.5
  36.6 0.0 copy-start.6
  36.6 0.0 copy-start.7
  36.6 86.5 %shard_map.122 = (f32[4,160,512]{2,1,0:T(8,128)}, f32[8,512]{1,0:T(8,128)S(1)}) custom-call(f32[160,1024]{1,0:T(8,128)} %copy-done.1, f32[160,1024]{1,0:T(8,128)} %copy-done.2, f32[160,1024]{1,0:T(8,128)} %copy-done.3, f32[160,1024]{1,0:T(8,128)} %copy-done.4, bf16[160,1024]{1,0:T(8,128)(2,1)S(1)} %get-tuple-element.17.refs_4_, ...), custom_call_target="tpu_custom_call" | custom-call | flops 17179869184 | bytes 8388608 | tf_op jit(solution)/shard_map/pallas_call | solution.py:256
  123.1 0.0 copy-done.5
  123.1 0.0 copy-done.6
  123.1 0.0 copy-done.7
  123.1 4.6 %fusion.2 = (f32[4,512,160]{1,2,0:T(8,128)}, f32[4,512,160]{1,2,0:T(8,128)}, f32[4,512,160]{1,2,0:T(8,128)}) fusion(f32[4,512,160]{1,2,0:T(8,128)S(1)} %copy-done.5, f32[4,160,512]{2,1,0:T(8,128)} %get-tuple-element.22, pred[4,512]{1,0:T(4,128)(4,1)S(1)} %slice_compare_fusion, f32[4,512,160]{1,2,0:T(8,128)S(1)} %copy-done.6, f32[4,512,160]{1,2,0:T(8,128)S(1)} %copy-done.7), kind=kLoop, calls=%fused_computation.6 | loop fusion | flops 5242880 | bytes 9177088 | tf_op jit(solution)/shard_map/transpose | solution.py:338
  (6 shorter events, 0.1 us)
Async XLA Ops:
  0.6 13.8 %copy-start = (f32[4,1280]{1,0:T(4,128)S(1)}, f32[4,1280]{1,0:T(4,128)}, u32[]{:S(2)}) copy-start(f32[4,1280]{1,0:T(4,128)} %taps_ref.1) | copy-start | bytes 61444
  1.4 10.1 %collective-permute-start.4 = (s32[4,1024]{1,0:T(4,128)S(1)}, s32[4,1024]{1,0:T(4,128)S(1)}, u32[]{:S(2)}, u32[]{:S(2)}) collective-permute-start(s32[4,1024]{1,0:T(4,128)S(1)} %bitcast_add_fusion), channel_id=1, source_target_pairs={{0,6},{2,4},{4,2},{6,0},{8,14},{10,12},{12,10},{14,8},{16,22},{18,... | collective-permute-start | bytes 49160 | tf_op jit(solution)/shard_map/ppermute | solution.py:28
  3.2 8.3 %collective-permute-start.3 = (s32[4,1024]{1,0:T(4,128)S(1)}, s32[4,1024]{1,0:T(4,128)S(1)}, u32[]{:S(2)}, u32[]{:S(2)}) collective-permute-start(s32[4,1024]{1,0:T(4,128)S(1)} %bitcast_add_fusion), channel_id=1, source_target_pairs={{0,4},{2,6},{4,0},{6,2},{8,12},{10,14},{12,8},{14,10},{16,20},{18,... | collective-permute-start | bytes 49160 | tf_op jit(solution)/shard_map/ppermute | solution.py:28
  3.5 8.0 %collective-permute-start.2 = (s32[4,1024]{1,0:T(4,128)S(1)}, s32[4,1024]{1,0:T(4,128)S(1)}, u32[]{:S(2)}, u32[]{:S(2)}) collective-permute-start(s32[4,1024]{1,0:T(4,128)S(1)} %bitcast_add_fusion), channel_id=1, source_target_pairs={{0,2},{2,0},{4,6},{6,4},{8,10},{10,8},{12,14},{14,12},{16,18},{18,... | collective-permute-start | bytes 49160 | tf_op jit(solution)/shard_map/ppermute | solution.py:28
  4.5 9.9 %collective-permute-start = (bf16[16,1280]{1,0:T(8,128)(2,1)S(1)}, bf16[16,1280]{1,0:T(8,128)(2,1)S(1)}, u32[]{:S(2)}, u32[]{:S(2)}) collective-permute-start(bf16[16,1280]{1,0:T(8,128)(2,1)S(1)} %get-tuple-element.27), channel_id=1, source_target_pairs={{0,2},{2,4},{4,6},{6,8},{8,10},{10,12},{12,14},{14,16},{16,18},{18... | collective-permute-start | bytes 122888 | tf_op jit(solution)/shard_map/ppermute | solution.py:24
  8.6 5.8 %collective-permute-start.1 = (bf16[2,16,1280]{2,1,0:T(8,128)(2,1)S(1)}, bf16[2,16,1280]{2,1,0:T(8,128)(2,1)S(1)}, u32[]{:S(2)}, u32[]{:S(2)}) collective-permute-start(bf16[2,16,1280]{2,1,0:T(8,128)(2,1)S(1)} %pad_maximum_fusion), channel_id=1, source_target_pairs={{2,0},{4,2},{6,4},{8,6},{10,8},{12,10},{14,12},{16,14},{18,16},{20... | collective-permute-start | bytes 245768 | tf_op jit(solution)/shard_map/ppermute | solution.py:24
  33.2 0.8 copy-start.1
  34.1 0.8 copy-start.2
  34.9 0.8 copy-start.3
  35.7 0.8 copy-start.4
  36.6 86.5 %copy-start.5 = (f32[4,512,160]{1,2,0:T(8,128)S(1)}, f32[4,512,160]{1,2,0:T(8,128)}, u32[]{:S(2)}) copy-start(f32[4,512,160]{1,2,0:T(8,128)} %param.19) | copy-start | bytes 3932164
  36.6 86.5 %copy-start.6 = (f32[4,512,160]{1,2,0:T(8,128)S(1)}, f32[4,512,160]{1,2,0:T(8,128)}, u32[]{:S(2)}) copy-start(f32[4,512,160]{1,2,0:T(8,128)} %param.18) | copy-start | bytes 3932164
  36.6 86.5 %copy-start.7 = (f32[4,512,160]{1,2,0:T(8,128)S(1)}, f32[4,512,160]{1,2,0:T(8,128)}, u32[]{:S(2)}) copy-start(f32[4,512,160]{1,2,0:T(8,128)} %param.17) | copy-start | bytes 3932164

commit v2 on v0

v2 whole, which is shorter than its diff:
```python
import functools

import jax
import jax.numpy as jnp
from jax import lax
from jax.experimental import pallas as pl
from jax.experimental.pallas import tpu as pltpu
from jax.sharding import PartitionSpec as P

beta_one = 0.9
beta_two = 0.95
learn_rate = 0.01
adam_steps = 10.0
epsilon = 1e-08
HALO = 16
GROUP = 4
ROWS_TILE = 128
LANES = 128
CONTRACT_LAST = (((1,), (1,)), ((), ()))


def conv_tile(context, upstream, gate, taps):
    reach, rows = upstream.shape[0], gate.shape[0]
    mixed = taps[0] * context[HALO : HALO + reach]
    for k in range(1, 4):
        mixed = mixed + taps[k] * context[HALO - 3 * k : HALO - 3 * k + reach]
    swing = 0.5 * jnp.tanh(0.5 * mixed)
    grad = upstream * (0.5 + swing) * (1.0 + mixed * (0.5 - swing))
    total = upstream[:rows]
    for k in range(4):
        total = total + taps[k] * grad[3 * k : 3 * k + rows]
    return (gate * total).astype(jnp.bfloat16)


def coded(values):
    peak = jnp.maximum(jnp.max(jnp.abs(values), axis=0, keepdims=True), 1e-30)
    steps = jnp.floor(values * (32766.0 / peak) + 0.5)
    return steps.astype(jnp.int32).astype(jnp.int16), peak * (1.0 / 32766.0)


def decoded(steps, scale):
    return steps.astype(jnp.int32).astype(jnp.float32) * scale


def layer_kernel(heads, tabs, planes, *refs):
    cot_ref, sv_ref, gate_ref, taps_ref, w_hbm, ids_ref, sums_ref, hits_ref = refs[:8]
    (
        w_ref, scaled, halos, ids_in, tab_out, tab_in, mine, core_in, side_in, diag_in, table_out, table_in, relayed,
        tab_scale_out, tab_scale_in, meta_out, meta_in, hit_sums, w_sem, halo_sems, ids_sems, tab_sems, tab_scale_sems,
        core_sems, side_sems, diag_sems, table_sems, meta_sems,
    ) = refs[8:]
    f32 = jnp.float32
    length, features = cot_ref.shape
    head_dim, rows = sums_ref.shape[1:]
    seqs = planes * GROUP
    seq, tab = lax.axis_index("seq"), lax.axis_index("tab")
    plane, column = seq // GROUP, seq % GROUP
    core = seq + 1 - 2 * (seq % 2)
    side = seq + 2 - 4 * ((seq // 2) % 2)
    diag = core + side - seq
    after, before = lax.rem(seq + 1, seqs), lax.rem(seq + seqs - 1, seqs)
    tab_peer = lambda k: lax.rem(tab + k, tabs)
    plane_peer = lambda k: lax.rem(plane + k, planes) * GROUP + column
    relays = planes == 4

    w_copy = pltpu.make_async_copy(w_hbm, w_ref, w_sem)
    w_copy.start()
    hits_ref[...] = jnp.zeros_like(hits_ref)
    barrier = pltpu.get_barrier_semaphore()

    def greet(**place):
        pl.semaphore_signal(barrier, inc=1, device_id=place, device_id_type=pl.DeviceIdType.MESH)

    for k in range(1, tabs):
        greet(tab=tab_peer(k))
    for peer in (core, side, diag, after, before):
        greet(seq=peer)
    for k in range(1, planes):
        greet(seq=plane_peer(k))
    pl.semaphore_wait(barrier, tabs + planes + 3)

    def copy(source, target, sems, place):
        return pltpu.make_async_remote_copy(
            src_ref=source,
            dst_ref=target,
            send_sem=sems.at[0],
            recv_sem=sems.at[1],
            device_id=place,
            device_id_type=pl.DeviceIdType.MESH,
        )

    halo_copies = [
        copy(sv_ref.at[pl.ds(length - HALO, HALO)], halos.at[0], halo_sems.at[0], {"seq": after}),
        copy(cot_ref.at[pl.ds(0, HALO)], halos.at[1], halo_sems.at[1], {"seq": before}),
        copy(sv_ref.at[pl.ds(0, HALO)], halos.at[2], halo_sems.at[2], {"seq": before}),
    ]
    ids_copies = [copy(ids_ref, ids_in.at[i], ids_sems.at[i], {"seq": p}) for i, p in enumerate((core, side, diag))]
    tab_copy = lambda k, h: copy(
        tab_out.at[k - 1, h], tab_in.at[k - 1, h], tab_sems.at[k - 1, h], {"tab": tab_peer(k)}
    )
    core_copy = lambda h: copy(mine.at[h], core_in.at[h], core_sems.at[h], {"seq": core})
    side_copy = lambda h: copy(mine.at[h], side_in.at[h], side_sems.at[h], {"seq": side})
    diag_copy = lambda h: copy(side_in.at[h], diag_in.at[h], diag_sems.at[h], {"seq": core})
    scale_copy = lambda k, h: copy(
        tab_scale_out.at[k - 1, h], tab_scale_in.at[k - 1, h], tab_scale_sems.at[k - 1, h], {"tab": tab_peer(k)}
    )

    def slot_copies(slot, h, target):
        return (
            copy(table_out.at[h, slot], table_in.at[h, slot], table_sems.at[h, slot], {"seq": target}),
            copy(meta_out.at[h, slot], meta_in.at[h, slot], meta_sems.at[h, slot], {"seq": target}),
        )

    def table_copies(k, h):
        return slot_copies(k - 1, h, plane_peer(k))

    def relay_copies(h):
        return slot_copies(1, h, lax.rem(2 * plane + 1, 5) * GROUP + column)

    def send(copies):
        for one in copies:
            one.start()

    def receive(copies):
        for one in copies:
            one.wait_recv()

    def put(h, slot, total, hits):
        table_out[h, slot], meta_out[h, slot, 0:1] = coded(total)
        meta_out[h, slot, 1:2] = hits

    def take(h, slot):
        return decoded(table_in[h, slot], meta_in[h, slot, 0:1]), meta_in[h, slot, 1:2]

    for started in halo_copies + ids_copies:
        started.start()

    tiles = length // ROWS_TILE

    def taps_at(lanes):
        return [taps_ref[k : k + 1, lanes] for k in range(4)]

    @pl.loop(0, features // LANES)
    def _(group):
        lanes = pl.ds(pl.multiple_of(group * LANES, LANES), LANES)
        taps = taps_at(lanes)

        @pl.loop(1, tiles - 1)
        def _(tile):
            start = pl.multiple_of(tile * ROWS_TILE, ROWS_TILE)
            behind = pl.multiple_of(tile * ROWS_TILE - HALO, HALO)
            context = sv_ref[pl.ds(behind, ROWS_TILE + 2 * HALO), lanes].astype(f32)
            upstream = cot_ref[pl.ds(start, ROWS_TILE + HALO), lanes].astype(f32)
            gate = gate_ref[pl.ds(start, ROWS_TILE), :]
            scaled[pl.ds(start, ROWS_TILE), lanes] = conv_tile(context, upstream, gate, taps)

    for arrived in halo_copies:
        arrived.wait()

    @pl.when(seq == 0)
    def _():
        halos[0] = jnp.zeros_like(halos[0])

    @pl.when(seq == seqs - 1)
    def _():
        halos[1] = jnp.zeros_like(halos[1])
        halos[2] = jnp.zeros_like(halos[2])

    @pl.loop(0, features // LANES)
    def _(group):
        lanes = pl.ds(pl.multiple_of(group * LANES, LANES), LANES)
        taps = taps_at(lanes)
        context = jnp.concatenate([halos[0, :, lanes], sv_ref[: ROWS_TILE + HALO, lanes]], axis=0).astype(f32)
        upstream = cot_ref[: ROWS_TILE + HALO, lanes].astype(f32)
        scaled[:ROWS_TILE, lanes] = conv_tile(context, upstream, gate_ref[:ROWS_TILE, :], taps)
        last = length - ROWS_TILE
        context = jnp.concatenate([sv_ref[last - HALO :, lanes], halos[2, :, lanes]], axis=0).astype(f32)
        upstream = jnp.concatenate([cot_ref[last:, lanes], halos[1, :, lanes]], axis=0).astype(f32)
        scaled[last:, lanes] = conv_tile(context, upstream, gate_ref[last:, :], taps)

    w_copy.wait()

    def part(away, h):
        first = pl.multiple_of((tab_peer(away) * heads + h) * head_dim, 32)
        return lax.dot_general(
            w_ref[pl.ds(first, head_dim), :], scaled[...], CONTRACT_LAST, preferred_element_type=f32
        )

    for h in range(heads):
        for k in range(1, tabs):
            tab_out[k - 1, h], tab_scale_out[k - 1, h] = coded(part(k, h))
            tab_copy(k, h).start()
            scale_copy(k, h).start()

    def combine(h):
        total = part(0, h)
        for k in range(1, tabs):
            tab_copy(k, h).wait_recv()
            scale_copy(k, h).wait_recv()
            total = total + decoded(tab_in[k - 1, h], tab_scale_in[k - 1, h])
        mine[h] = total.astype(jnp.bfloat16)
        side_copy(h).start()
        core_copy(h).start()

    def forward(h):
        side_copy(h).wait_recv()
        diag_copy(h).start()

    middle, final = (3 - 2 * (plane // 2), 1 + 2 * (plane // 2)) if relays else (0, 0)
    edge = 1 - ((plane + 1) // 2) % 2

    def add_up(h):
        core_copy(h).wait_recv()
        diag_copy(h).wait_recv()
        row = lax.broadcasted_iota(jnp.int32, (rows, length), 0)
        ones = jnp.ones((16, length), jnp.bfloat16)

        def sums_of(away):
            first = plane_peer(away) * rows
            total = jnp.zeros((head_dim + 16, rows), f32)
            for source, held in enumerate((mine, core_in, side_in, diag_in)):
                ids = ids_ref[h : h + 1, :] if source == 0 else ids_in[source - 1, h : h + 1, :]
                chosen = (ids - first == row).astype(f32).astype(jnp.bfloat16)
                grads = jnp.concatenate([held[h], ones], axis=0)
                total = total + lax.dot_general(grads, chosen, CONTRACT_LAST, preferred_element_type=f32)
            return total[:head_dim], total[head_dim : head_dim + 1]

        if relays:
            put(h, 1, *sums_of(2))
            send(relay_copies(h))
            put(h, middle - 1, *sums_of(middle))
            send(table_copies(middle, h))
            relayed[h], hit_sums[h] = sums_of(final)

            @pl.when(edge == 1)
            def _():
                put(h, final - 1, relayed[h], hit_sums[h])
                send(table_copies(final, h))

        else:

            @pl.loop(1, planes)
            def _(away):
                put(h, away - 1, *sums_of(away))
                send(table_copies(away, h))

        sums_ref[h], hits_ref[h] = sums_of(0)

    def relay(h):
        @pl.when(edge == 0)
        def _():
            receive(relay_copies(h))
            total, hits = take(h, 1)
            put(h, final - 1, relayed[h] + total, hit_sums[h] + hits)
            send(table_copies(final, h))

    def collect(h, slot):
        total, hits = take(h, slot)
        sums_ref[h] = sums_ref[h] + total
        hits_ref[h] = hits_ref[h] + hits

    combine(0)
    for arrived in ids_copies:
        arrived.wait()
    for h in range(heads):
        if h + 1 < heads:
            combine(h + 1)
        forward(h)
        add_up(h)
        if relays and h > 0:
            relay(h - 1)
    if relays:
        relay(heads - 1)

    for h in range(heads):
        if relays:
            for k in (1, 3):
                receive(table_copies(k, h))
                collect(h, k - 1)

            @pl.when(edge == 1)
            def _():
                receive(relay_copies(h))
                collect(h, 1)

        else:
            for k in range(1, planes):
                receive(table_copies(k, h))
                collect(h, k - 1)
    for h in range(heads):
        for k in range(1, tabs):
            tab_copy(k, h).wait_send()
            scale_copy(k, h).wait_send()
        side_copy(h).wait_send()
        core_copy(h).wait_send()
        diag_copy(h).wait_send()
        for k in range(1, planes):
            for one in table_copies(k, h):
                one.wait_send()


def layer(cotangent, saved_value, gate, taps, weight, ids, rows, head_dim, tabs, planes):
    heads, length = ids.shape
    features = cotangent.shape[1]
    vmem = pl.BlockSpec(memory_space=pltpu.VMEM)
    bf16, f32 = jnp.bfloat16, jnp.float32
    block = (heads, head_dim, length)
    tables = (heads, planes - 1, head_dim, rows)
    pairs = lambda *shape: pltpu.SemaphoreType.DMA((*shape, 2))
    return pl.pallas_call(
        functools.partial(layer_kernel, heads, tabs, planes),
        out_shape=[
            jax.ShapeDtypeStruct((heads, head_dim, rows), f32),
            jax.ShapeDtypeStruct((heads, 1, rows), f32),
        ],
        in_specs=[vmem, vmem, vmem, vmem, pl.BlockSpec(memory_space=pl.ANY), vmem],
        out_specs=[vmem, vmem],
        scratch_shapes=[
            pltpu.VMEM(weight.shape, bf16),
            pltpu.VMEM((length, features), bf16),
            pltpu.VMEM((3, HALO, features), bf16),
            pltpu.VMEM((3, heads, length), jnp.int32),
            pltpu.VMEM((max(tabs - 1, 1), *block), jnp.int16),
            pltpu.VMEM((max(tabs - 1, 1), *block), jnp.int16),
            pltpu.VMEM(block, bf16),
            pltpu.VMEM(block, bf16),
            pltpu.VMEM(block, bf16),
            pltpu.VMEM(block, bf16),
            pltpu.VMEM(tables, jnp.int16),
            pltpu.VMEM(tables, jnp.int16),
            pltpu.VMEM((heads, head_dim, rows), f32),
            pltpu.VMEM((max(tabs - 1, 1), heads, 1, length), f32),
            pltpu.VMEM((max(tabs - 1, 1), heads, 1, length), f32),
            pltpu.VMEM((heads, planes - 1, 2, rows), f32),
            pltpu.VMEM((heads, planes - 1, 2, rows), f32),
            pltpu.VMEM((heads, 1, rows), f32),
            pltpu.SemaphoreType.DMA,
            pairs(3),
            pairs(3),
            pairs(max(tabs - 1, 1), heads),
            pairs(max(tabs - 1, 1), heads),
            pairs(heads),
            pairs(heads),
            pairs(heads),
            pairs(heads, planes - 1),
            pairs(heads, planes - 1),
        ],
        compiler_params=pltpu.CompilerParams(
            vmem_limit_bytes=56 * 1024 * 1024, collective_id=0, has_side_effects=True
        ),
    )(cotangent, saved_value, gate, taps, weight, ids)


def shards(
    cotangent,
    saved_value,
    gate_scale,
    conv_weight,
    value_weight,
    owner_ids,
    local_row,
    row_table,
    moment_one,
    moment_two,
):
    heads, rows, head_dim = row_table.shape
    tabs, planes = lax.axis_size("tab"), lax.axis_size("seq") // GROUP
    ids = owner_ids[:, :, 0] * rows + local_row
    row_grad, hits = layer(
        cotangent, saved_value, gate_scale[:, None], conv_weight, value_weight, ids, rows, head_dim, tabs, planes
    )
    touched = hits > 0
    turned = lambda array: jnp.swapaxes(array, 1, 2)
    table, first, second = turned(row_table), turned(moment_one), turned(moment_two)
    first_next = beta_one * first + (1.0 - beta_one) * row_grad
    second_next = beta_two * second + (1.0 - beta_two) * row_grad * row_grad
    update = (
        first_next
        / (1.0 - beta_one**adam_steps)
        / (jnp.sqrt(second_next / (1.0 - beta_two**adam_steps)) + epsilon)
    )
    table_next = table - learn_rate * update
    return (
        turned(jnp.where(touched, table_next, table)),
        turned(jnp.where(touched, first_next, first)),
        turned(jnp.where(touched, second_next, second)),
    )


def solution(mesh):
    in_specs = (
        P("seq", "tab"),
        P("seq", "tab"),
        P("seq"),
        P(None, "tab"),
        P(None, "tab"),
        P("tab", "seq", None),
        P("tab", "seq"),
        P("tab", "seq", None),
        P("tab", "seq", None),
        P("tab", "seq", None),
    )
    out_specs = (P("tab", "seq", None), P("tab", "seq", None), P("tab", "seq", None))
    return jax.shard_map(shards, mesh=mesh, in_specs=in_specs, out_specs=out_specs, check_vma=False)
```

time: 582 us -> 96.2 us (0.17)
  waiting for transfers between devices: 245 us -> 0 us
  other arithmetic: 193 us -> 6.55 us
  local copies, waits for them, and re-layouts: 90.4 us -> 1.72 us
  Pallas kernels: 0 us -> 86.8 us
  starting transfers between devices: 18.3 us -> 0 us
  matrix products: 17.3 us -> 0 us
  between operations: 14.3 us -> 0.68 us
    unnamed x9 -> x0, other arithmetic: 177 us -> none
    all_to_all x2 -> x0, waiting for transfers between devices: 137 us -> none  [the longest x1 137 us: shards(): lax.all_to_all(send_grad, 'seq', split_axis=1, concat_axis=1, tiled=True)]
    psum x1 -> x0, waiting for transfers between devices: 104 us -> none  [shards(): summed = lax.psum(full_term, 'tab')]
    pallas_call x0 -> x1, Pallas kernels: none -> 86.8 us  [layer(): pl.pallas_call(functools.partial(layer_kernel, heads, tabs, planes), out_...]
    unnamed x30 -> x7, local copies, waits for them, and re-layouts: 47.6 us -> 0.02 us
    reshape x4 -> x0, local copies, waits for them, and re-layouts: 30.6 us -> none  [the longest x1 15.4 us: shards(): send_grad = send_grad.reshape(head_local, peer_count, count_cap, head_dim)]
    dot_general x1 -> x0, matrix products: 17.3 us -> none  [shards(): lax.dot_general(value_weight, scaled, (((1,), (1,)), ((), ())), preferred...]
    all_to_all x2 -> x0, starting transfers between devices: 12.5 us -> none  [the longest x1 6.53 us: shards(): lax.all_to_all(send_grad, 'seq', split_axis=1, concat_axis=1, tiled=True)]
  transfers between devices with their start and end apart: 5 -> 0, of which waited for: 3 -> 0; matrix products, arithmetic and copies ran while one was open for 28% -> 0% of each run, Pallas kernels for 0% -> 0%
where the time goes in v2:
time: 96.2 us; the launch traced here: 95.7 us
  Pallas kernels  86.8 us (90%)
  other arithmetic  6.55 us (7%)
  local copies, waits for them, and re-layouts  1.72 us (2%)
    pallas_call x1, Pallas kernels, layer(): pl.pallas_call(functools.partial(layer_kernel, heads, tabs, planes), out_...  86.8 us
    transpose x1, other arithmetic, shards(): turned = lambda array: jnp.swapaxes(array, 1, 2)  4.49 us

profile of v2, /device:TPU:9, one launch (start us, length us, event | category | flops | bytes accessed | tf_op | source)
XLA Modules:
  0.0 95.7 jit_solution(12523796232014310406)
XLA Ops:
  0.6 1.3 %bitcast_add_fusion.refs_5_ = s32[4,1024]{1,0:T(4,128)} fusion(s32[4,1024]{1,0:T(4,128)} %param.16, s32[4,1024,1]{1,2,0:T(1,128)} %param.15), kind=kLoop, calls=%fused_computation.11 | loop fusion | flops 8192 | bytes 49152 | tf_op jit(solution)/shard_map/add | solution.py:368
  2.0 1.7 %copy.15.refs_2_ = f32[1024,1]{1,0:T(8,128)} copy(f32[1024,1]{0,1:T(1,128)} %bitcast.37) | data formatting | bytes 8192 | tf_op jit(solution)/shard_map/broadcast_in_dim | solution.py:370
  3.7 0.0 copy-start
  3.7 0.0 copy-start.1
  3.7 0.0 copy-start.2
  3.7 86.8 %shard_map.121 = (f32[4,160,512]{2,1,0:T(8,128)}, f32[4,1,512]{2,1,0:T(1,128)}) custom-call(bf16[1024,1280]{1,0:T(8,128)(2,1)} %refs_0_.1, bf16[1024,1280]{1,0:T(8,128)(2,1)} %refs_1_.1, f32[1024,1]{1,0:T(8,128)} %copy.15.refs_2_, f32[4,1280]{1,0:T(4,128)} %refs_3_.1, bf16[1280,1280]{1,0:T(8,128)(2,1)} %refs_4_.1, s32[4,1024]{1,0:T(4,128)} %bitcast_add_fusion.refs_5_), custom_call_target="tpu_custom_call" | custom-call | tf_op jit(solution)/shard_map/pallas_call | solution.py:310
  90.5 0.7 broadcast_compare_fusion
  91.2 0.0 copy-done
  91.2 0.0 copy-done.1
  91.2 0.0 copy-done.2
  91.2 4.5 %fusion.2 = (f32[4,512,160]{1,2,0:T(8,128)}, f32[4,512,160]{1,2,0:T(8,128)}, f32[4,512,160]{1,2,0:T(8,128)}) fusion(f32[4,512,160]{1,2,0:T(8,128)S(1)} %copy-done, f32[4,160,512]{2,1,0:T(8,128)} %get-tuple-element.6, pred[4,512]{1,0:T(4,128)(4,1)S(1)} %bitcast.36, f32[4,512,160]{1,2,0:T(8,128)S(1)} %copy-done.1, f32[4,512,160]{1,2,0:T(8,128)S(1)} %copy-done.2), kind=kLoop, calls=%fused_computation.6 | loop fusion | flops 5242880 | bytes 9177088 | tf_op jit(solution)/shard_map/transpose | solution.py:373
  (1 shorter events, 0.0 us)
Async XLA Ops:
  3.7 87.5 %copy-start = (f32[4,512,160]{1,2,0:T(8,128)S(1)}, f32[4,512,160]{1,2,0:T(8,128)}, u32[]{:S(2)}) copy-start(f32[4,512,160]{1,2,0:T(8,128)} %param.19) | copy-start | bytes 3932164
  3.7 87.5 %copy-start.1 = (f32[4,512,160]{1,2,0:T(8,128)S(1)}, f32[4,512,160]{1,2,0:T(8,128)}, u32[]{:S(2)}) copy-start(f32[4,512,160]{1,2,0:T(8,128)} %param.18) | copy-start | bytes 3932164
  3.7 87.5 %copy-start.2 = (f32[4,512,160]{1,2,0:T(8,128)S(1)}, f32[4,512,160]{1,2,0:T(8,128)}, u32[]{:S(2)}) copy-start(f32[4,512,160]{1,2,0:T(8,128)} %param.17) | copy-start | bytes 3932164
